TPU v7x, 256 devices: a whole 4x4x8 slice. The times are simulated.
256 devices in a mesh: sta: 32 (over z, y), freq: 8 (over x, core).
Axes of the slice: x: 4, y: 4, z: 8, core: 2. Of those that a mesh axis runs over, the one named last changes fastest.
Arguments:
- spectra: bfloat16 [8, 2048, 2, 4096], P(None, 'sta', None, 'freq'), may hold values from -6 to 6
- pair_blocks: int32 [32, 2], P('sta'), may hold values from 0 to 31, as said below
Outputs:
- correlations: float32 [64, 32, 64, 1024], P('freq', 'sta')
Inputs may be any that keep to these rules, and one draw needn't show every extreme that they name: `pair_blocks`: in every row the first block is smaller than the second, and both lie within 4 blocks of the row's owner p; the first row of each owner pairs the lowest and the highest block of that range.
All inputs are finite; a program needn't handle non-finite values.
Results may differ from a plain program's by a relative error of at most 0.0037.
Values may be sent and summed in bfloat16 or wider, within the bound.
A program may use at most 128 MiB of HBM per device.

v0:
```python
import math

import jax
import jax.numpy as jnp
from jax import lax
from jax.sharding import PartitionSpec as P

LAGS = 1024
WIN = 8


def shifted(value, axis, steps):
    count = lax.axis_size(axis)
    leading, last = (max(0, -steps), min(count, count - steps))
    return lax.ppermute(value, axis, [(source, source + steps) for source in range(leading, last)])


def table_rows(row_start, bin_count, lag_count, fft_length):
    bin_index = row_start + lax.iota(jnp.int32, bin_count)
    lag_offset = lax.iota(jnp.int32, lag_count) - lag_count // 2
    phase_index = bin_index[:, None] * lag_offset[None, :] % fft_length
    angles = phase_index.astype(jnp.float32) * (2.0 * math.pi / fft_length)
    return jnp.concatenate([jnp.cos(angles), -jnp.sin(angles)], 0).astype(jnp.bfloat16)


def on_device(spectra, pair_blocks):
    reach_blocks = min(4, lax.axis_size("sta") // 4)
    bins_local = spectra.shape[3]
    freq_parts = lax.axis_size("freq")
    bins_total = bins_local * freq_parts
    fft_length = 2 * bins_total
    norm_factor = 1.0 / math.sqrt(WIN * bins_total)
    below = []
    above = []

    def fetch_far(offset_blocks):
        return shifted(spectra, "sta", -offset_blocks)

    for distance in range(1, reach_blocks + 1):
        above.append(fetch_far(distance))
        below.insert(0, fetch_far(-distance))
    window = jnp.stack(below + [spectra] + above)
    position = lax.axis_index("sta")
    first_slot = pair_blocks[:, 0] - position + reach_blocks
    second_slot = pair_blocks[:, 1] - position + reach_blocks
    left_blocks = jnp.take(window, first_slot, axis=0)
    right_blocks = jnp.take(window, second_slot, axis=0)
    turned = jnp.stack([-right_blocks[:, :, :, 1], right_blocks[:, :, :, 0]], axis=3)
    real_part = jnp.einsum(
        "pwacf,pwbcf->apbf", left_blocks, right_blocks, preferred_element_type=jnp.float32
    )
    imag_part = jnp.einsum(
        "pwacf,pwbcf->apbf", left_blocks, turned, preferred_element_type=jnp.float32
    )
    cross_spec = jnp.stack([real_part, imag_part], axis=3).astype(jnp.bfloat16)
    block_in = lax.all_to_all(cross_spec, "freq", split_axis=0, concat_axis=4, tiled=True)
    rows_here = block_in.shape[0]
    pair_count = block_in.shape[1]
    columns = block_in.shape[2]

    def add_slice(running, slice_index):
        row_start = slice_index * bins_local
        bin_piece = lax.dynamic_slice_in_dim(block_in, row_start, bins_local, 4)
        dft_table = table_rows(row_start, bins_local, LAGS, fft_length)
        flat_rows = bin_piece.reshape(-1, 2 * bins_local)
        return (running + jnp.dot(flat_rows, dft_table, preferred_element_type=jnp.float32), None)

    start_sum = jnp.zeros((rows_here * pair_count * columns, LAGS), jnp.float32)
    running, unused = lax.scan(add_slice, start_sum, lax.iota(jnp.int32, freq_parts))
    summed = running.reshape(rows_here, pair_count, columns, LAGS)
    return summed * norm_factor


def solution(mesh):
    return jax.shard_map(
        on_device,
        mesh=mesh,
        in_specs=(P(None, "sta", None, "freq"), P("sta", None)),
        out_specs=P("freq", "sta", None, None),
        check_vma=False,
    )
```

profile of v0, /device:TPU:112, one launch (start us, length us, event | category | flops | bytes accessed | tf_op | source)
XLA Modules:
  0.0 467.2 jit_solution(18100134890920147558)
XLA Ops:
  0.0 2.5 copy.35
  2.5 5.2 %collective-permute-start = (bf16[8,64,2,512]{3,1,2,0:T(8,128)(2,1)}, bf16[8,64,2,512]{3,1,2,0:T(8,128)(2,1)}, u32[]{:S(2)}, u32[]{:S(2)}) collective-permute-start(bf16[8,64,2,512]{3,1,2,0:T(8,128)(2,1)} %copy.35), channel_id=1, source_target_pairs={{0,32},{8,40},{16,48},{24,56},{32,64},{40,72},{48,80},{56,88},{64,... | collective-permute-start | bytes 3145736 | tf_op jit(solution)/shard_map/ppermute | solution.py:15
  7.7 2.8 collective-permute-start.1
  10.5 4.8 %collective-permute-start.2 = (bf16[8,64,2,512]{3,1,2,0:T(8,128)(2,1)}, bf16[8,64,2,512]{3,1,2,0:T(8,128)(2,1)}, u32[]{:S(2)}, u32[]{:S(2)}) collective-permute-start(bf16[8,64,2,512]{3,1,2,0:T(8,128)(2,1)} %copy.35), channel_id=1, source_target_pairs={{0,16},{8,24},{16,32},{24,40},{32,48},{40,56},{48,64},{56,72},{64,... | collective-permute-start | bytes 3145736 | tf_op jit(solution)/shard_map/ppermute | solution.py:15
  15.3 2.0 collective-permute-start.3
  17.3 3.9 collective-permute-start.4
  21.2 2.6 copy.43
  25.8 5.8 %collective-permute-done = bf16[8,64,2,512]{3,1,2,0:T(8,128)(2,1)} collective-permute-done((bf16[8,64,2,512]{3,1,2,0:T(8,128)(2,1)}, bf16[8,64,2,512]{3,1,2,0:T(8,128)(2,1)}, u32[]{:S(2)}, u32[]{:S(2)}) %collective-permute-start) | collective-permute-done | bytes 1048608 | tf_op jit(solution)/shard_map/ppermute | solution.py:15
  33.4 3.8 copy.36
  37.2 16.9 %collective-permute-done.1 = bf16[8,64,2,512]{3,1,2,0:T(8,128)(2,1)} collective-permute-done((bf16[8,64,2,512]{3,1,2,0:T(8,128)(2,1)}, bf16[8,64,2,512]{3,1,2,0:T(8,128)(2,1)}, u32[]{:S(2)}, u32[]{:S(2)}) %collective-permute-start.1) | collective-permute-done | bytes 1048608 | tf_op jit(solution)/shard_map/ppermute | solution.py:15
  54.2 50.5 %collective-permute-start.6 = (bf16[8,64,2,512]{3,1,2,0:T(8,128)(2,1)}, bf16[8,64,2,512]{3,1,2,0:T(8,128)(2,1)}, u32[]{:S(2)}, u32[]{:S(2)}) collective-permute-start(bf16[8,64,2,512]{3,1,2,0:T(8,128)(2,1)} %copy.35), channel_id=1, source_target_pairs={{24,0},{32,8},{40,16},{48,24},{56,32},{64,40},{72,48},{80,56},{88,... | collective-permute-start | bytes 3145736 | tf_op jit(solution)/shard_map/ppermute | solution.py:15
  104.6 3.8 copy.38
  108.5 3.4 bitcast_dynamic-update-slice_fusion.8
  113.6 2.0 collective-permute-start.7
  115.6 3.8 copy.40
  119.4 3.8 copy.42
  123.3 3.5 bitcast_dynamic-update-slice_fusion.6
  130.2 3.0 copy.45
  133.2 2.8 copy.47
  136.0 3.8 copy.49
  146.0 7.4 %collective-permute-done.7 = bf16[8,64,2,512]{3,1,2,0:T(8,128)(2,1)} collective-permute-done((bf16[8,64,2,512]{3,1,2,0:T(8,128)(2,1)}, bf16[8,64,2,512]{3,1,2,0:T(8,128)(2,1)}, u32[]{:S(2)}, u32[]{:S(2)}) %collective-permute-start.7) | collective-permute-done | bytes 1048608 | tf_op jit(solution)/shard_map/ppermute | solution.py:15
  153.4 3.2 copy.51
  160.3 4.1 fusion.10
  164.5 7.5 %fusion.11 = bf16[64,1,64,1,512]{0,2,4,3,1:T(8,128)(2,1)} fusion(bf16[1,8,64,1,512]{2,1,3,4,0:T(8,128)(2,1)S(1)} %get-tuple-element.107, bf16[1,8,64,1,512]{2,1,3,4,0:T(8,128)(2,1)S(1)} %get-tuple-element.106, bf16[9,8,64,2,512]{2,1,3,4,0:T(8,128)(2,1)} %bitcast_dynamic-update-slice_fusion, s32[]{:T(128)} %bitcast.16, pred[]{:T(512)} %bitcast.15), kind=kOutput, calls=%fused_computation.23 | convolution fusion | flops 70254592 | bytes 7341056 | tf_op jit(solution)/shard_map/pwacf,pwbcf->apbf/dot_general | solution.py:52
  172.0 11.7 %pad_maximum_fusion = bf16[64,1,64,2,512]{0,2,4,3,1:T(8,128)(2,1)} fusion(bf16[64,1,64,1,512]{0,2,4,3,1:T(8,128)(2,1)} %fusion.11, bf16[64,1,64,1,512]{0,2,4,3,1:T(8,128)(2,1)S(1)} %fusion.10), kind=kLoop, calls=%fused_computation.19 | loop fusion | flops 4194304 | bytes 16777216 | tf_op jit(solution)/shard_map/stack | solution.py:55
  183.7 22.3 %copy.52 = bf16[64,1,64,2,512]{4,2,3,1,0:T(8,128)(2,1)} copy(bf16[64,1,64,2,512]{0,2,4,3,1:T(8,128)(2,1)} %pad_maximum_fusion) | data formatting | bytes 16777216 | tf_op jit(solution)/shard_map/stack | solution.py:55
  206.0 5.2 %all-to-all-start = ((bf16[64,1,64,2,512]{4,2,3,1,0:T(8,128)(2,1)}), bf16[64,1,64,2,512]{4,2,3,1,0:T(8,128)(2,1)}, u32[]{:S(2)}, u32[]{:S(2)}) async-start(bf16[64,1,64,2,512]{4,2,3,1,0:T(8,128)(2,1)} %copy.52), calls=%async_computation | async-start | bytes 16777216 | tf_op jit(solution)/shard_map/all_to_all | solution.py:56
  211.2 94.4 %all-to-all-done = bf16[64,1,64,2,512]{4,2,3,1,0:T(8,128)(2,1)} async-done(((bf16[64,1,64,2,512]{4,2,3,1,0:T(8,128)(2,1)}), bf16[64,1,64,2,512]{4,2,3,1,0:T(8,128)(2,1)}, u32[]{:S(2)}, u32[]{:S(2)}) %all-to-all-start) | async-done | bytes 8388640 | tf_op jit(solution)/shard_map/all_to_all | solution.py:56
  305.6 11.9 %copy.57 = bf16[8,1,64,2,8,512]{5,4,3,2,0,1:T(8,128)(2,1)} copy(bf16[8,1,64,2,8,512]{5,2,3,1,0,4:T(8,128)(2,1)} %bitcast.30) | data formatting | bytes 16777216
  317.5 14.5 %reshape.146 = bf16[8,1,64,2,4096]{4,3,2,1,0:T(2,128)(2,1)} reshape(bf16[8,1,64,2,8,512]{5,4,3,2,0,1:T(8,128)(2,1)} %copy.57) | data formatting | bytes 16777216
  332.0 131.9 %while.14 = (s32[]{:T(128)}, f32[512,1024]{1,0:T(8,128)}, s32[8]{0:T(128)S(1)}, bf16[8,1,64,2,4096]{4,3,2,1,0:T(2,128)(2,1)}, s32[]{:T(128)}, /*index=5*/s32[1]{0:T(128)}, s32[]{:T(128)}, s32[]{:T(128)}) while((s32[]{:T(128)}, f32[512,1024]{1,0:T(8,128)}, s32[8]{0:T(128)S(1)}, bf16[8,1,64,2,4096]{4,3,2,1,0:T(2,128)(2,1)}, ...), condition=%wide.region_1.3_spmd.clone, body=%wide.region_0.0_spmd.clone.sunk | while | flops 1087899136 | bytes 13643937 | solution.py:69
  335.5 9.0 %cosine_convert_fusion.2 = (bf16[512,1024]{1,0:T(8,128)(2,1)S(1)}, bf16[512,1024]{1,0:T(8,128)(2,1)S(1)}) fusion(s32[1024]{0:T(1024)S(1)} %iota_add_fusion.4, s32[512]{0:T(512)S(1)} %iota_add_fusion.5), kind=kLoop, calls=%fused_computation.14.clone.1 | loop fusion | flops 8912896 | bytes 2103296 | tf_op jit(solution)/shard_map/convert
  344.5 2.6 select_add_fusion.2
  350.6 9.0 %cosine_convert_fusion.2 = (bf16[512,1024]{1,0:T(8,128)(2,1)S(1)}, bf16[512,1024]{1,0:T(8,128)(2,1)S(1)}) fusion(s32[1024]{0:T(1024)S(1)} %iota_add_fusion.4, s32[512]{0:T(512)S(1)} %iota_add_fusion.5), kind=kLoop, calls=%fused_computation.14.clone.1 | loop fusion | flops 8912896 | bytes 2103296 | tf_op jit(solution)/shard_map/convert
  359.6 4.2 select_add_fusion.2
  367.3 9.0 %cosine_convert_fusion.2 = (bf16[512,1024]{1,0:T(8,128)(2,1)S(1)}, bf16[512,1024]{1,0:T(8,128)(2,1)S(1)}) fusion(s32[1024]{0:T(1024)S(1)} %iota_add_fusion.4, s32[512]{0:T(512)S(1)} %iota_add_fusion.5), kind=kLoop, calls=%fused_computation.14.clone.1 | loop fusion | flops 8912896 | bytes 2103296 | tf_op jit(solution)/shard_map/convert
  376.3 4.2 select_add_fusion.2
  383.9 9.0 %cosine_convert_fusion.2 = (bf16[512,1024]{1,0:T(8,128)(2,1)S(1)}, bf16[512,1024]{1,0:T(8,128)(2,1)S(1)}) fusion(s32[1024]{0:T(1024)S(1)} %iota_add_fusion.4, s32[512]{0:T(512)S(1)} %iota_add_fusion.5), kind=kLoop, calls=%fused_computation.14.clone.1 | loop fusion | flops 8912896 | bytes 2103296 | tf_op jit(solution)/shard_map/convert
  393.0 4.2 select_add_fusion.2
  400.6 9.0 %cosine_convert_fusion.2 = (bf16[512,1024]{1,0:T(8,128)(2,1)S(1)}, bf16[512,1024]{1,0:T(8,128)(2,1)S(1)}) fusion(s32[1024]{0:T(1024)S(1)} %iota_add_fusion.4, s32[512]{0:T(512)S(1)} %iota_add_fusion.5), kind=kLoop, calls=%fused_computation.14.clone.1 | loop fusion | flops 8912896 | bytes 2103296 | tf_op jit(solution)/shard_map/convert
  409.7 4.2 select_add_fusion.2
  417.3 9.0 %cosine_convert_fusion.2 = (bf16[512,1024]{1,0:T(8,128)(2,1)S(1)}, bf16[512,1024]{1,0:T(8,128)(2,1)S(1)}) fusion(s32[1024]{0:T(1024)S(1)} %iota_add_fusion.4, s32[512]{0:T(512)S(1)} %iota_add_fusion.5), kind=kLoop, calls=%fused_computation.14.clone.1 | loop fusion | flops 8912896 | bytes 2103296 | tf_op jit(solution)/shard_map/convert
  426.4 4.2 select_add_fusion.2
  434.0 9.0 %cosine_convert_fusion.2 = (bf16[512,1024]{1,0:T(8,128)(2,1)S(1)}, bf16[512,1024]{1,0:T(8,128)(2,1)S(1)}) fusion(s32[1024]{0:T(1024)S(1)} %iota_add_fusion.4, s32[512]{0:T(512)S(1)} %iota_add_fusion.5), kind=kLoop, calls=%fused_computation.14.clone.1 | loop fusion | flops 8912896 | bytes 2103296 | tf_op jit(solution)/shard_map/convert
  443.0 4.2 select_add_fusion.2
  450.7 9.0 %cosine_convert_fusion.2 = (bf16[512,1024]{1,0:T(8,128)(2,1)S(1)}, bf16[512,1024]{1,0:T(8,128)(2,1)S(1)}) fusion(s32[1024]{0:T(1024)S(1)} %iota_add_fusion.4, s32[512]{0:T(512)S(1)} %iota_add_fusion.5), kind=kLoop, calls=%fused_computation.14.clone.1 | loop fusion | flops 8912896 | bytes 2103296 | tf_op jit(solution)/shard_map/convert
  459.7 4.2 select_add_fusion.2
  463.9 3.3 broadcast_multiply_fusion
  (70 shorter events, 40.0 us)
Async XLA Ops:
  0.0 21.2 %copy-start.4 = (bf16[8,64,2,512]{3,2,1,0:T(2,128)(2,1)S(1)}, bf16[8,64,2,512]{3,2,1,0:T(2,128)(2,1)}, u32[]{:S(2)}) copy-start(bf16[8,64,2,512]{3,2,1,0:T(2,128)(2,1)} %param.6) | copy-start | bytes 3145732
  2.5 21.3 %copy-start.5 = (s32[1,2]{1,0:T(1,128)S(1)}, s32[1,2]{1,0:T(1,128)}, u32[]{:S(2)}) copy-start(s32[1,2]{1,0:T(1,128)} %param.7) | copy-start | bytes 28
  2.5 29.0 %collective-permute-start = (bf16[8,64,2,512]{3,1,2,0:T(8,128)(2,1)}, bf16[8,64,2,512]{3,1,2,0:T(8,128)(2,1)}, u32[]{:S(2)}, u32[]{:S(2)}) collective-permute-start(bf16[8,64,2,512]{3,1,2,0:T(8,128)(2,1)} %copy.35), channel_id=1, source_target_pairs={{0,32},{8,40},{16,48},{24,56},{32,64},{40,72},{48,80},{56,88},{64,... | collective-permute-start | bytes 3145736 | tf_op jit(solution)/shard_map/ppermute | solution.py:15
  7.7 46.5 %collective-permute-start.1 = (bf16[8,64,2,512]{3,1,2,0:T(8,128)(2,1)}, bf16[8,64,2,512]{3,1,2,0:T(8,128)(2,1)}, u32[]{:S(2)}, u32[]{:S(2)}) collective-permute-start(bf16[8,64,2,512]{3,1,2,0:T(8,128)(2,1)} %copy.35), channel_id=1, source_target_pairs={{0,24},{8,32},{16,40},{24,48},{32,56},{40,64},{48,72},{56,80},{64,... | collective-permute-start | bytes 3145736 | tf_op jit(solution)/shard_map/ppermute | solution.py:15
  10.5 103.1 %collective-permute-start.2 = (bf16[8,64,2,512]{3,1,2,0:T(8,128)(2,1)}, bf16[8,64,2,512]{3,1,2,0:T(8,128)(2,1)}, u32[]{:S(2)}, u32[]{:S(2)}) collective-permute-start(bf16[8,64,2,512]{3,1,2,0:T(8,128)(2,1)} %copy.35), channel_id=1, source_target_pairs={{0,16},{8,24},{16,32},{24,40},{32,48},{40,56},{48,64},{56,72},{64,... | collective-permute-start | bytes 3145736 | tf_op jit(solution)/shard_map/ppermute | solution.py:15
  15.3 104.1 %collective-permute-start.3 = (bf16[8,64,2,512]{3,1,2,0:T(8,128)(2,1)}, bf16[8,64,2,512]{3,1,2,0:T(8,128)(2,1)}, u32[]{:S(2)}, u32[]{:S(2)}) collective-permute-start(bf16[8,64,2,512]{3,1,2,0:T(8,128)(2,1)} %copy.35), channel_id=1, source_target_pairs={{0,8},{8,16},{16,24},{24,32},{32,40},{40,48},{48,56},{56,64},{64,7... | collective-permute-start | bytes 3145736 | tf_op jit(solution)/shard_map/ppermute | solution.py:15
  17.3 112.9 %collective-permute-start.4 = (bf16[8,64,2,512]{3,1,2,0:T(8,128)(2,1)}, bf16[8,64,2,512]{3,1,2,0:T(8,128)(2,1)}, u32[]{:S(2)}, u32[]{:S(2)}) collective-permute-start(bf16[8,64,2,512]{3,1,2,0:T(8,128)(2,1)} %copy.35), channel_id=1, source_target_pairs={{8,0},{16,8},{24,16},{32,24},{40,32},{48,40},{56,48},{64,56},{72,6... | collective-permute-start | bytes 3145736 | tf_op jit(solution)/shard_map/ppermute | solution.py:15
  31.5 101.7 %collective-permute-start.5 = (bf16[8,64,2,512]{3,1,2,0:T(8,128)(2,1)}, bf16[8,64,2,512]{3,1,2,0:T(8,128)(2,1)S(1)}, u32[]{:S(2)}, u32[]{:S(2)}) collective-permute-start(bf16[8,64,2,512]{3,1,2,0:T(8,128)(2,1)} %copy.35), channel_id=1, source_target_pairs={{16,0},{24,8},{32,16},{40,24},{48,32},{56,40},{64,48},{72,56},{80,... | collective-permute-start | bytes 3145736 | tf_op jit(solution)/shard_map/ppermute | solution.py:15
  54.2 81.9 %collective-permute-start.6 = (bf16[8,64,2,512]{3,1,2,0:T(8,128)(2,1)}, bf16[8,64,2,512]{3,1,2,0:T(8,128)(2,1)}, u32[]{:S(2)}, u32[]{:S(2)}) collective-permute-start(bf16[8,64,2,512]{3,1,2,0:T(8,128)(2,1)} %copy.35), channel_id=1, source_target_pairs={{24,0},{32,8},{40,16},{48,24},{56,32},{64,40},{72,48},{80,56},{88,... | collective-permute-start | bytes 3145736 | tf_op jit(solution)/shard_map/ppermute | solution.py:15
  108.5 3.4 copy-start.3
  113.6 39.8 %collective-permute-start.7 = (bf16[8,64,2,512]{3,1,2,0:T(8,128)(2,1)}, bf16[8,64,2,512]{3,1,2,0:T(8,128)(2,1)}, u32[]{:S(2)}, u32[]{:S(2)}) collective-permute-start(bf16[8,64,2,512]{3,1,2,0:T(8,128)(2,1)} %copy.35), channel_id=1, source_target_pairs={{32,0},{40,8},{48,16},{56,24},{64,32},{72,40},{80,48},{88,56},{96,... | collective-permute-start | bytes 3145736 | tf_op jit(solution)/shard_map/ppermute | solution.py:15
  123.3 3.5 copy-start.2
  139.9 2.2 copy-start
  142.1 2.2 copy-start.1
  206.0 99.6 %all-to-all-start = ((bf16[64,1,64,2,512]{4,2,3,1,0:T(8,128)(2,1)}), bf16[64,1,64,2,512]{4,2,3,1,0:T(8,128)(2,1)}, u32[]{:S(2)}, u32[]{:S(2)}) async-start(bf16[64,1,64,2,512]{4,2,3,1,0:T(8,128)(2,1)} %copy.52), calls=%async_computation | async-start | bytes 16777216 | tf_op jit(solution)/shard_map/all_to_all | solution.py:56
where the time goes:
time: 470 us; the launch traced here: 467 us
  local copies, waits for them, and re-layouts  125 us (27%)
  waiting for transfers between devices  125 us (27%)
  other arithmetic  89.3 us (19%)
  starting transfers between devices  78.2 us (17%)
  matrix products  43.5 us (9%)
  loops' own time  5.47 us (1%)
    all_to_all x1, waiting for transfers between devices, on_device(): lax.all_to_all(cross_spec, 'freq', split_axis=0, concat_axis=4, tiled=True)  94.4 us
    ppermute x8, starting transfers between devices, shifted(): lax.ppermute(value, axis, [(source, source + steps) for source in range(l...  73 us
    another operation x8, other arithmetic  72.2 us
    unnamed x24, local copies, waits for them, and re-layouts  49.6 us
    dot_general x8, matrix products, add_slice(): jnp.dot(flat_rows, dft_table, preferred_element_type=jnp.float32)  31.8 us
    ppermute x8, waiting for transfers between devices, shifted(): lax.ppermute(value, axis, [(source, source + steps) for source in range(l...  30.1 us
    ppermute x8, local copies, waits for them, and re-layouts, shifted(): lax.ppermute(value, axis, [(source, source + steps) for source in range(l...  28.1 us
    another operation x1, local copies, waits for them, and re-layouts, on_device(): cross_spec = jnp.stack([real_part, imag_part], axis=3).astype(jnp.bfloat16)  22.3 us
  transfers between devices with their start and end apart: 9, of which 4 were waited for; matrix products, arithmetic and copies ran while one was open for 10% of the time, Pallas kernels for 0%

commit v1 on v0

v1 whole, which is shorter than its diff:
```python
import functools
import math

import jax
import jax.numpy as jnp
import ml_dtypes
import numpy as np
from jax import lax
from jax.experimental import pallas as pl
from jax.experimental.pallas import tpu as pltpu
from jax.sharding import PartitionSpec as P

LAGS = 1024
WIN = 8
BLK = 64
NY = 4
LANES = 128
MESH = pl.DeviceIdType.MESH
F32 = jnp.float32
BF16 = jnp.bfloat16

SOURCES = ((0, 0), (0, 1), (1, 0), (3, 0), (1, 1), (3, 1), (2, 0), (2, 1))


def table_pieces(parts, steps, bins_total):
    fft_length = 2 * bins_total
    bins = np.arange(bins_total, dtype=np.int64)
    lags = np.arange(LAGS, dtype=np.int64) - LAGS // 2
    angles = ((bins[:, None] * lags[None, :]) % fft_length) * (2.0 * math.pi / fft_length)
    both = np.stack([np.cos(angles), -np.sin(angles)]).astype(np.float32)
    both = both.reshape(2, parts, steps, LANES, LAGS).transpose(1, 2, 0, 3, 4)
    return both.reshape(parts, steps, 2 * LANES, LAGS).astype(ml_dtypes.bfloat16)


def kernel(rows_z, steps, norm, s_ref, t_ref, o_ref, y_buf, x_in, x_buf, table, lhs, xf,
           xz_sem, yz_sem, y_sem, x_sem, t_sem, xo_sem, yo_sem, xe_sem, ye_sem, ys_sem, xs_sem):
    sta = lax.axis_index("sta")
    me = lax.axis_index("freq")
    z = sta // NY
    yy = sta % NY
    chip = me // 2
    core = me % 2
    last = rows_z * NY - 1
    up = (me + 2) % 8
    down = (me + 6) % 8
    mate = me + 1 - 2 * core

    def peer(dr, ds):
        return 2 * ((chip + dr) % 4) + (core + ds) % 2

    x_low = z == 0
    y_high = z == rows_z - 1
    x_src = sta == 0
    y_src = sta == last
    x_pass = jnp.logical_and(x_low, yy % 2 == 1)
    y_pass = jnp.logical_and(y_high, yy % 2 == 0)
    x_half = jnp.where(yy == 1, 0, 4)
    y_half = jnp.where(yy == 2, 0, 4)

    barrier = pltpu.get_barrier_semaphore()

    def greet(row, col):
        pl.semaphore_signal(barrier, inc=1, device_id=(row, col), device_id_type=MESH)

    for dr, ds in SOURCES[1:]:
        greet(sta, peer(dr, ds))

    @pl.when(z > 0)
    def _():
        greet(sta - NY, me)

    @pl.when(z < rows_z - 1)
    def _():
        greet(sta + NY, me)

    @pl.when(x_pass)
    def _():
        greet(0, me)

    @pl.when(jnp.logical_and(x_low, yy == 2))
    def _():
        greet(1, me)
        greet(3, me)

    @pl.when(y_pass)
    def _():
        greet(last, me)

    @pl.when(jnp.logical_and(y_high, yy == 1))
    def _():
        greet(last - 1, me)
        greet(last - 3, me)

    expected = 7
    for flag, count in ((z < rows_z - 1, 1), (z > 0, 1), (x_src, 2), (y_src, 2), (x_pass, 1), (y_pass, 1)):
        expected = expected + jnp.where(flag, count, 0)
    pl.semaphore_wait(barrier, expected)

    def remote(src, dst, send, recv, row, col):
        return pltpu.make_async_remote_copy(
            src_ref=src, dst_ref=dst, send_sem=send, recv_sem=recv,
            device_id=(row, col), device_id_type=MESH)

    def x_out(t):
        return remote(s_ref.at[t], x_in.at[t], xo_sem.at[t], xz_sem.at[t], sta + NY, me)

    def y_out(t):
        return remote(s_ref.at[t], y_buf.at[0, 0, t], yo_sem.at[t], yz_sem.at[t], sta - NY, me)

    def x_edge(t, n):
        return remote(s_ref.at[t], x_in.at[t], xe_sem.at[t, n], xz_sem.at[t], 1 + 2 * n, me)

    def y_edge(t, n):
        return remote(s_ref.at[t], y_buf.at[0, 0, t], ye_sem.at[t, n], yz_sem.at[t], last - 1 - 2 * n, me)

    def x_own(t):
        return pltpu.make_async_copy(s_ref.at[t], x_in.at[t], xz_sem.at[t])

    def y_own(t):
        return pltpu.make_async_copy(s_ref.at[t], y_buf.at[0, 0, t], yz_sem.at[t])

    def x_relay(t):
        piece = x_in.at[t, pl.ds(x_half, 4)]
        return remote(piece, piece, xe_sem.at[t, 0], xz_sem.at[t], 2, me)

    def y_relay(t):
        piece = y_buf.at[0, 0, t, pl.ds(y_half, 4)]
        return remote(piece, piece, ye_sem.at[t, 0], yz_sem.at[t], last - 2, me)

    def y_copy(t, n, src, dst, col, lo=0, size=8):
        return remote(y_buf.at[src[0], src[1], t, pl.ds(lo, size)], y_buf.at[dst[0], dst[1], t, pl.ds(lo, size)],
                      ys_sem.at[t, n], y_sem.at[dst[0], dst[1], t], sta, col)

    def y_first(t):
        return (y_copy(t, 0, (0, 0), (3, 0), up), y_copy(t, 1, (0, 0), (1, 0), down),
                y_copy(t, 2, (0, 0), (0, 1), mate))

    def y_second(t):
        return (y_copy(t, 3, (3, 0), (2, 0), up, 0, 4), y_copy(t, 4, (3, 0), (3, 1), mate),
                y_copy(t, 5, (1, 0), (2, 0), down, 4, 4), y_copy(t, 6, (1, 0), (1, 1), mate))

    def y_third(t):
        return (y_copy(t, 7, (2, 0), (2, 1), mate),)

    def x_copies(t):
        return [
            remote(x_in.at[t, peer(dr, ds)], x_buf.at[(4 - dr) % 4, ds, t], xs_sem.at[t, n],
                   x_sem.at[(4 - dr) % 4, ds, t], sta, peer(dr, ds))
            for n, (dr, ds) in enumerate(SOURCES) if n]

    def x_mine(t):
        return pltpu.make_async_copy(x_in.at[t, me], x_buf.at[0, 0, t], x_sem.at[0, 0, t])

    def arrived(ref, sem):
        pltpu.make_async_copy(ref, ref, sem).wait()

    def table_copy(t, n):
        dr, ds = SOURCES[n]
        return pltpu.make_async_copy(t_ref.at[peer(dr, ds), t], table.at[t, pl.ds(2 * LANES * n, 2 * LANES)],
                                     t_sem.at[t, n])

    def each_start(t, start):
        def go(copy):
            if start:
                copy.start()
            else:
                copy.wait_send()

        @pl.when(z < rows_z - 1)
        def _():
            go(x_out(t))

        @pl.when(z > 0)
        def _():
            go(y_out(t))

        @pl.when(x_src)
        def _():
            go(x_edge(t, 0))
            go(x_edge(t, 1))
            if start:
                x_own(t).start()

        @pl.when(y_src)
        def _():
            go(y_edge(t, 0))
            go(y_edge(t, 1))
            if start:
                y_own(t).start()

    def enter(t):
        arrived(y_buf.at[0, 0, t], yz_sem.at[t])
        for copy in y_first(t):
            copy.start()

        @pl.when(y_pass)
        def _():
            y_relay(t).start()

        arrived(x_in.at[t], xz_sem.at[t])
        x_mine(t).start()
        for copy in x_copies(t):
            copy.start()

        @pl.when(x_pass)
        def _():
            x_relay(t).start()

    def cross(t, n):
        r, s = SOURCES[n]
        arrived(x_buf.at[r, s, t], x_sem.at[r, s, t])
        xf[...] = x_buf[r, s, t].astype(F32)

        def body(j, carry):
            pair = []
            for h in range(2):
                v = y_buf[r, s, t, 2 * j + h].astype(F32)
                pair.append((v[0].reshape(WIN, 8, LANES), v[1].reshape(WIN, 8, LANES)))
            for a in range(8):
                reals = []
                imags = []
                for yr, yi in pair:
                    re = im = None
                    for w in range(WIN):
                        xr = xf[0, pl.ds(w * 8 + a, 1), :]
                        xi = xf[1, pl.ds(w * 8 + a, 1), :]
                        p = xr * yr[w] + xi * yi[w]
                        q = xi * yr[w] - xr * yi[w]
                        re = p if re is None else re + p
                        im = q if im is None else im + q
                    reals.append(re)
                    imags.append(im)
                rows = pl.ds(pl.multiple_of(a * BLK + 16 * j, 16), 16)
                at = 2 * LANES * n
                lhs[rows, at:at + LANES] = jnp.concatenate(reals, 0).astype(BF16)
                lhs[rows, at + LANES:at + 2 * LANES] = jnp.concatenate(imags, 0).astype(BF16)
            return carry

        lax.fori_loop(0, 4, body, 0)

    def all_tables(t, carry):
        for n in range(8):
            table_copy(t, n).start()
        return carry

    def all_out(t, carry):
        each_start(t, True)
        return carry

    lax.fori_loop(0, steps, all_out, 0)
    lax.fori_loop(0, steps, all_tables, 0)
    enter(0)
    o_ref[...] = jnp.zeros_like(o_ref)

    def step(t, carry):
        cross(t, 0)

        @pl.when(t < steps - 1)
        def _():
            enter(t + 1)

        arrived(y_buf.at[0, 1, t], y_sem.at[0, 1, t])
        cross(t, 1)
        arrived(y_buf.at[3, 0, t], y_sem.at[3, 0, t])
        arrived(y_buf.at[1, 0, t], y_sem.at[1, 0, t])
        for copy in y_second(t):
            copy.start()
        cross(t, 2)
        cross(t, 3)
        arrived(y_buf.at[1, 1, t], y_sem.at[1, 1, t])
        cross(t, 4)
        arrived(y_buf.at[2, 0, t], y_sem.at[2, 0, t])
        for copy in y_third(t):
            copy.start()
        arrived(y_buf.at[3, 1, t], y_sem.at[3, 1, t])
        cross(t, 5)
        cross(t, 6)
        arrived(y_buf.at[2, 1, t], y_sem.at[2, 1, t])
        cross(t, 7)
        for n in range(8):
            table_copy(t, n).wait()

        def columns(i, inner):
            cols = pl.ds(pl.multiple_of(i * 256, 256), 256)
            o_ref[:, cols] += jnp.dot(lhs[...], table[t, :, cols], preferred_element_type=F32) * norm
            return inner

        lax.fori_loop(0, LAGS // 256, columns, 0)
        return carry

    lax.fori_loop(0, steps, step, 0)

    def drain(t, carry):
        each_start(t, False)

        @pl.when(x_pass)
        def _():
            x_relay(t).wait_send()

        @pl.when(y_pass)
        def _():
            y_relay(t).wait_send()

        for copy in y_first(t) + y_second(t) + y_third(t):
            copy.wait_send()
        for copy in x_copies(t):
            copy.wait_send()
        return carry

    lax.fori_loop(0, steps, drain, 0)


def on_device(rows_z, parts, spectra, pair_blocks):
    del pair_blocks
    bins_local = spectra.shape[3]
    steps = bins_local // LANES
    bins_total = bins_local * parts
    norm = 1.0 / math.sqrt(WIN * bins_total)
    table = jnp.asarray(table_pieces(parts, steps, bins_total))
    pieces = spectra.reshape(WIN, 8, 8, 2, steps, LANES).transpose(4, 1, 3, 0, 2, 5)
    pieces = pieces.reshape(steps, 8, 2, BLK, LANES)
    dma = pltpu.SemaphoreType.DMA
    out = pl.pallas_call(
        functools.partial(kernel, rows_z, steps, norm),
        out_shape=jax.ShapeDtypeStruct((8 * BLK, LAGS), F32),
        in_specs=[pl.BlockSpec(memory_space=pl.ANY)] * 2,
        out_specs=pl.BlockSpec(memory_space=pltpu.VMEM),
        scratch_shapes=[
            pltpu.VMEM((4, 2, steps, 8, 2, BLK, LANES), BF16),
            pltpu.VMEM((steps, 8, 2, BLK, LANES), BF16),
            pltpu.VMEM((4, 2, steps, 2, BLK, LANES), BF16),
            pltpu.VMEM((steps, 16 * LANES, LAGS), BF16),
            pltpu.VMEM((8 * BLK, 16 * LANES), BF16),
            pltpu.VMEM((2, BLK, LANES), F32),
            dma((steps,)), dma((steps,)), dma((4, 2, steps)), dma((4, 2, steps)), dma((steps, 8)),
            dma((steps,)), dma((steps,)), dma((steps, 2)), dma((steps, 2)), dma((steps, 8)), dma((steps, 8)),
        ],
        compiler_params=pltpu.CompilerParams(
            collective_id=0, has_side_effects=True, vmem_limit_bytes=52 * 1024 * 1024),
        cost_estimate=pl.CostEstimate(flops=9_000_000_000, bytes_accessed=24_000_000, transcendentals=0),
    )(pieces, table)
    return out.reshape(8, 1, BLK, LAGS)


def solution(mesh):
    rows_z = mesh.shape["sta"] // NY
    return jax.shard_map(
        functools.partial(on_device, rows_z, mesh.shape["freq"]),
        mesh=mesh,
        in_specs=(P(None, "sta", None, "freq"), P("sta", None)),
        out_specs=P("freq", "sta", None, None),
        check_vma=False,
    )
```

time: 470 us -> 103 us (0.22)
  the two profiles are of different devices: /device:TPU:112 before, /device:TPU:232 now
where the time goes in v1:
time: 103 us; the launch traced here: 102 us
  Pallas kernels  96.7 us (94%)
  local copies, waits for them, and re-layouts  5.14 us (5%)
    pallas_call x1, Pallas kernels, on_device(): pl.pallas_call(functools.partial(kernel, rows_z, steps, norm), out_shape=...  96.7 us
    unnamed x1, local copies, waits for them, and re-layouts  3.16 us

profile of v1, /device:TPU:232, one launch (start us, length us, event | category | flops | bytes accessed | tf_op | source)
XLA Modules:
  0.0 101.9 jit_solution(6025295093277270749)
XLA Ops:
  0.0 1.7 %reshape.9 = bf16[8,8,8,2,4,128]{5,4,3,2,1,0:T(4,128)(2,1)S(1)} reshape(bf16[8,64,2,512]{3,2,1,0:T(2,128)(2,1)} %param.3) | data formatting | bytes 2097152 | tf_op jit(solution)/shard_map/reshape | solution.py:320
  1.7 0.3 copy.6
  2.0 96.7 %shard_map.28 = f32[512,1024]{1,0:T(8,128)} custom-call(bf16[4,8,2,64,128]{4,3,2,1,0:T(8,128)(2,1)S(1)} %bitcast.8, bf16[8,4,256,1024]{3,2,1,0:T(8,128)(2,1)} %constant.2.clone.t_ref), custom_call_target="tpu_custom_call" | custom-call | flops 8999999488 | bytes 24000000 | tf_op jit(solution)/shard_map/pallas_call | solution.py:323
  98.7 3.2 %copy.8 = f32[8,1,64,1024]{3,2,1,0:T(8,128)} copy(f32[8,1,64,1024]{3,2,1,0:T(8,128)} %bitcast.9) | data formatting | bytes 4194304

commit v2 on v1

v2 whole, which is shorter than its diff:
```python
import functools
import math

import jax
import jax.numpy as jnp
import ml_dtypes
import numpy as np
from jax import lax
from jax.experimental import pallas as pl
from jax.experimental.pallas import tpu as pltpu
from jax.sharding import PartitionSpec as P

LAGS = 1024
WIN = 8
BLK = 64
NY = 4
LANES = 128
MESH = pl.DeviceIdType.MESH
F32 = jnp.float32
BF16 = jnp.bfloat16

OWN, MATE, FAR, FARMATE = range(4)


def table_pieces(parts, steps, bins_total):
    fft_length = 2 * bins_total
    bins = np.arange(bins_total, dtype=np.int64)
    lags = np.arange(LAGS, dtype=np.int64) - LAGS // 2
    angles = ((bins[:, None] * lags[None, :]) % fft_length) * (2.0 * math.pi / fft_length)
    both = np.stack([np.cos(angles), -np.sin(angles)]).astype(np.float32)
    both = both.reshape(2, parts, steps, LANES, LAGS).transpose(1, 2, 0, 3, 4)
    return both.reshape(parts, steps, 2 * LANES, LAGS).astype(ml_dtypes.bfloat16)


def kernel(rows_z, steps, norm, s_ref, t_ref, o_ref, y_buf, x_in, x_buf, table, lhs, xf, acc, r_out, r_in,
           xz_sem, yz_sem, y_sem, x_sem, t_sem, xo_sem, yo_sem, xe_sem, ye_sem, ys_sem, xs_sem, ro_sem, ri_sem):
    sta = lax.axis_index("sta")
    me = lax.axis_index("freq")
    z = sta // NY
    yy = sta % NY
    chip = me // 2
    core = me % 2
    last = rows_z * NY - 1
    turn = 1 - 2 * (chip % 2)
    side = ((chip + turn + 4) % 4, (chip - turn + 4) % 4)
    across = (chip + 2) % 4
    mate = me + 1 - 2 * core

    def at(where, other):
        return 2 * where + (core + other) % 2

    x_low = z == 0
    y_high = z == rows_z - 1
    x_src = sta == 0
    y_src = sta == last
    x_pass = jnp.logical_and(x_low, yy % 2 == 1)
    y_pass = jnp.logical_and(y_high, yy % 2 == 0)
    x_half = jnp.where(yy == 1, 0, 4)
    y_half = jnp.where(yy == 2, 0, 4)

    barrier = pltpu.get_barrier_semaphore()

    def greet(row, col):
        pl.semaphore_signal(barrier, inc=1, device_id=(row, col), device_id_type=MESH)

    greet(sta, mate)
    for h in range(2):
        for other in range(2):
            greet(sta, at(side[h], other))

    @pl.when(z > 0)
    def _():
        greet(sta - NY, me)

    @pl.when(z < rows_z - 1)
    def _():
        greet(sta + NY, me)

    @pl.when(x_pass)
    def _():
        greet(0, me)

    @pl.when(jnp.logical_and(x_low, yy == 2))
    def _():
        greet(1, me)
        greet(3, me)

    @pl.when(y_pass)
    def _():
        greet(last, me)

    @pl.when(jnp.logical_and(y_high, yy == 1))
    def _():
        greet(last - 1, me)
        greet(last - 3, me)

    expected = 5
    for flag, count in ((z < rows_z - 1, 1), (z > 0, 1), (x_src, 2), (y_src, 2), (x_pass, 1), (y_pass, 1)):
        expected = expected + jnp.where(flag, count, 0)
    pl.semaphore_wait(barrier, expected)

    def remote(src, dst, send, recv, row, col):
        return pltpu.make_async_remote_copy(
            src_ref=src, dst_ref=dst, send_sem=send, recv_sem=recv,
            device_id=(row, col), device_id_type=MESH)

    def x_out(t):
        return remote(s_ref.at[t], x_in.at[t], xo_sem.at[t], xz_sem.at[t], sta + NY, me)

    def y_out(t):
        return remote(s_ref.at[t], y_buf.at[OWN, t], yo_sem.at[t], yz_sem.at[t], sta - NY, me)

    def x_edge(t, n):
        return remote(s_ref.at[t], x_in.at[t], xe_sem.at[t, n], xz_sem.at[t], 1 + 2 * n, me)

    def y_edge(t, n):
        return remote(s_ref.at[t], y_buf.at[OWN, t], ye_sem.at[t, n], yz_sem.at[t], last - 1 - 2 * n, me)

    def x_own(t):
        return pltpu.make_async_copy(s_ref.at[t], x_in.at[t], xz_sem.at[t])

    def y_own(t):
        return pltpu.make_async_copy(s_ref.at[t], y_buf.at[OWN, t], yz_sem.at[t])

    def x_relay(t):
        piece = x_in.at[t, pl.ds(x_half, 4)]
        return remote(piece, piece, xe_sem.at[t, 0], xz_sem.at[t], 2, me)

    def y_relay(t):
        piece = y_buf.at[OWN, t, pl.ds(y_half, 4)]
        return remote(piece, piece, ye_sem.at[t, 0], yz_sem.at[t], last - 2, me)

    def y_sides(t):
        return [remote(y_buf.at[OWN, t, pl.ds(4 * h, 4)], y_buf.at[FAR, t, pl.ds(4 * h, 4)], ys_sem.at[t, h],
                       y_sem.at[FAR, t], sta, at(side[h], 0)) for h in range(2)]

    def y_mate(t):
        return remote(y_buf.at[OWN, t], y_buf.at[MATE, t], ys_sem.at[t, 2], y_sem.at[MATE, t], sta, mate)

    def y_far(t):
        return remote(y_buf.at[FAR, t], y_buf.at[FARMATE, t], ys_sem.at[t, 3], y_sem.at[FARMATE, t], sta, mate)

    def x_sides(t):
        copies = []
        for h in range(2):
            for g, where in enumerate((side[h], across)):
                for other in range(2):
                    source = FAR + other
                    copies.append(remote(
                        x_in.at[t, at(where, other)], x_buf.at[source, t, 2 * h + g], xs_sem.at[t, 4 * h + 2 * g + other],
                        x_sem.at[source, t], sta, at(side[h], other)))
        return copies

    def x_mate(t):
        return [remote(x_in.at[t, at((chip, side[1], chip, side[0])[q], 1)], x_buf.at[MATE, t, q], xs_sem.at[t, 8 + q],
                       x_sem.at[MATE, t], sta, mate) for q in range(4)]

    def x_mine(t):
        return [pltpu.make_async_copy(x_in.at[t, at((chip, side[1], chip, side[0])[q], 0)], x_buf.at[OWN, t, q],
                                      xs_sem.at[t, 12 + q]) for q in range(4)]

    def arrived(ref, sem):
        pltpu.make_async_copy(ref, ref, sem).wait()

    def table_copy(t, n):
        chunk = at((side[0], chip, side[1])[n // 2], n % 2)
        return pltpu.make_async_copy(t_ref.at[chunk, t], table.at[t, pl.ds(2 * LANES * n, 2 * LANES)], t_sem.at[t, n])

    def each_start(t, start):
        def go(copy):
            if start:
                copy.start()
            else:
                copy.wait_send()

        @pl.when(z < rows_z - 1)
        def _():
            go(x_out(t))

        @pl.when(z > 0)
        def _():
            go(y_out(t))

        @pl.when(x_src)
        def _():
            go(x_edge(t, 0))
            go(x_edge(t, 1))
            if start:
                x_own(t).start()

        @pl.when(y_src)
        def _():
            go(y_edge(t, 0))
            go(y_edge(t, 1))
            if start:
                y_own(t).start()

    def enter(t):
        arrived(y_buf.at[OWN, t], yz_sem.at[t])
        for copy in y_sides(t):
            copy.start()
        y_mate(t).start()

        @pl.when(y_pass)
        def _():
            y_relay(t).start()

        arrived(x_in.at[t], xz_sem.at[t])
        for copy in x_sides(t) + x_mate(t) + x_mine(t):
            copy.start()

        @pl.when(x_pass)
        def _():
            x_relay(t).start()

    def second(t):
        arrived(y_buf.at[FAR, t], y_sem.at[FAR, t])
        y_far(t).start()

    def cross(t, src, g):
        for h in range(2):
            x = x_buf[src, t, 2 * h + g].astype(F32)
            xf[h, 0] = x[0]
            xf[h, 1] = x[1]
            xf[h, 2] = x[0] + x[1]

        for h in range(2):
            def body(j, carry, h=h):
                pair = []
                for k in range(2):
                    v = y_buf[src, t, 4 * h + 2 * j + k].astype(F32)
                    yr = v[0].reshape(WIN, 8, LANES)
                    yi = v[1].reshape(WIN, 8, LANES)
                    pair.append((yr, yi, yr - yi))
                for a in range(8):
                    reals = []
                    imags = []
                    for yr, yi, yd in pair:
                        u = v = d = None
                        for w in range(WIN):
                            row = pl.ds(w * 8 + a, 1)
                            uw = xf[h, 0, row, :] * yr[w]
                            vw = xf[h, 1, row, :] * yi[w]
                            dw = xf[h, 2, row, :] * yd[w]
                            u = uw if u is None else u + uw
                            v = vw if v is None else v + vw
                            d = dw if d is None else d + dw
                        reals.append(u + v)
                        imags.append(d - (u - v))
                    rows = pl.ds(pl.multiple_of(a * 32 + 16 * j, 16), 16)
                    col = 2 * LANES * ((src + 2 - 2 * h) % 4)
                    lhs[h, rows, col:col + LANES] = jnp.concatenate(reals, 0).astype(BF16)
                    lhs[h, rows, col + LANES:col + 2 * LANES] = jnp.concatenate(imags, 0).astype(BF16)
                return carry

            lax.fori_loop(0, 2, body, 0)

    def product(t, h):
        return jnp.dot(lhs[h], table[t, 4 * LANES * h:4 * LANES * h + 8 * LANES, :], preferred_element_type=F32)

    def r_copy(h):
        return remote(r_out.at[h], r_in.at[h], ro_sem.at[h], ri_sem.at[h], sta, at(side[1 - h], 0))

    def all_out(t, carry):
        each_start(t, True)
        return carry

    def all_tables(t, carry):
        for n in range(6):
            table_copy(t, n).start()
        return carry

    lax.fori_loop(0, steps, all_out, 0)
    lax.fori_loop(0, steps, all_tables, 0)
    acc[...] = jnp.zeros_like(acc)

    def near(t):
        for copy in x_mine(t):
            copy.wait()
        cross(t, OWN, 1)
        arrived(y_buf.at[MATE, t], y_sem.at[MATE, t])
        arrived(x_buf.at[MATE, t], x_sem.at[MATE, t])
        cross(t, MATE, 1)

    def far(t):
        second(t)
        arrived(x_buf.at[FAR, t], x_sem.at[FAR, t])
        cross(t, FAR, 1)
        arrived(y_buf.at[FARMATE, t], y_sem.at[FARMATE, t])
        arrived(x_buf.at[FARMATE, t], x_sem.at[FARMATE, t])
        cross(t, FARMATE, 1)
        for n in range(6):
            table_copy(t, n).wait()

    enter(0)
    near(0)

    def step(t, carry):
        enter(t)
        far(t - 1)
        for h in range(2):
            acc[1, h] += product(t - 1, h)
        near(t)
        return carry

    lax.fori_loop(1, steps, step, 0)
    far(steps - 1)
    for h in range(2):
        r_out[h] = (acc[1, h] + product(steps - 1, h)).astype(BF16)
        r_copy(h).start()

    def mine(t, carry):
        for src in range(4):
            cross(t, src, 0)
        for h in range(2):
            acc[0, h] += product(t, h)
        return carry

    lax.fori_loop(0, steps, mine, 0)

    for h in range(2):
        r_copy(h).wait_recv()
        total = (acc[0, h] + r_in[h].astype(F32)) * norm
        o_ref[:, 32 * h:32 * h + 32, :] = total.reshape(8, 32, LAGS)

    def drain(t, carry):
        each_start(t, False)

        @pl.when(x_pass)
        def _():
            x_relay(t).wait_send()

        @pl.when(y_pass)
        def _():
            y_relay(t).wait_send()

        for copy in y_sides(t) + [y_mate(t), y_far(t)] + x_sides(t) + x_mate(t):
            copy.wait_send()
        return carry

    lax.fori_loop(0, steps, drain, 0)
    for h in range(2):
        r_copy(h).wait_send()


def on_device(rows_z, parts, spectra, pair_blocks):
    del pair_blocks
    bins_local = spectra.shape[3]
    steps = bins_local // LANES
    bins_total = bins_local * parts
    norm = 1.0 / math.sqrt(WIN * bins_total)
    table = jnp.asarray(table_pieces(parts, steps, bins_total))
    pieces = spectra.reshape(WIN, 8, 8, 2, steps, LANES).transpose(4, 1, 3, 0, 2, 5)
    pieces = pieces.reshape(steps, 8, 2, BLK, LANES)
    dma = pltpu.SemaphoreType.DMA
    out = pl.pallas_call(
        functools.partial(kernel, rows_z, steps, norm),
        out_shape=jax.ShapeDtypeStruct((8, BLK, LAGS), F32),
        in_specs=[pl.BlockSpec(memory_space=pl.ANY)] * 2,
        out_specs=pl.BlockSpec(memory_space=pltpu.VMEM),
        scratch_shapes=[
            pltpu.VMEM((4, steps, 8, 2, BLK, LANES), BF16),
            pltpu.VMEM((steps, 8, 2, BLK, LANES), BF16),
            pltpu.VMEM((4, steps, 4, 2, BLK, LANES), BF16),
            pltpu.VMEM((steps, 12 * LANES, LAGS), BF16),
            pltpu.VMEM((2, 256, 8 * LANES), BF16),
            pltpu.VMEM((2, 3, BLK, LANES), F32),
            pltpu.VMEM((2, 2, 256, LAGS), F32),
            pltpu.VMEM((2, 256, LAGS), BF16),
            pltpu.VMEM((2, 256, LAGS), BF16),
            dma((steps,)), dma((steps,)), dma((4, steps)), dma((4, steps)), dma((steps, 6)),
            dma((steps,)), dma((steps,)), dma((steps, 2)), dma((steps, 2)), dma((steps, 4)), dma((steps, 16)),
            dma((2,)), dma((2,)),
        ],
        compiler_params=pltpu.CompilerParams(
            collective_id=0, has_side_effects=True, vmem_limit_bytes=52 * 1024 * 1024),
        cost_estimate=pl.CostEstimate(flops=9_000_000_000, bytes_accessed=24_000_000, transcendentals=0),
    )(pieces, table)
    return out.reshape(8, 1, BLK, LAGS)


def solution(mesh):
    rows_z = mesh.shape["sta"] // NY
    return jax.shard_map(
        functools.partial(on_device, rows_z, mesh.shape["freq"]),
        mesh=mesh,
        in_specs=(P(None, "sta", None, "freq"), P("sta", None)),
        out_specs=P("freq", "sta", None, None),
        check_vma=False,
    )
```

time: 103 us -> 64.1 us (0.62)
  Pallas kernels: 96.7 us -> 58.8 us
    pallas_call x1, Pallas kernels: 96.7 us -> 58.8 us  [on_device(): pl.pallas_call(functools.partial(kernel, rows_z, steps, norm), out_shape=...]
where the time goes in v2:
time: 64.1 us; the launch traced here: 64 us
  Pallas kernels  58.8 us (92%)
  local copies, waits for them, and re-layouts  5.14 us (8%)
    pallas_call x1, Pallas kernels, on_device(): pl.pallas_call(functools.partial(kernel, rows_z, steps, norm), out_shape=...  58.8 us
    unnamed x1, local copies, waits for them, and re-layouts  3.16 us
    reshape x2, local copies, waits for them, and re-layouts, on_device(): spectra.reshape(WIN, 8, 8, 2, steps, LANES).transpose(4, 1, 3, 0, 2, 5)  1.99 us

profile of v2, /device:TPU:232, one launch (start us, length us, event | category | flops | bytes accessed | tf_op | source)
XLA Modules:
  0.0 64.0 jit_solution(5165943193543448161)
XLA Ops:
  0.0 1.7 %reshape.9 = bf16[8,8,8,2,4,128]{5,4,3,2,1,0:T(4,128)(2,1)S(1)} reshape(bf16[8,64,2,512]{3,2,1,0:T(2,128)(2,1)} %param.3) | data formatting | bytes 2097152 | tf_op jit(solution)/shard_map/reshape | solution.py:353
  1.7 0.3 copy.6
  2.0 58.8 %shard_map.28 = f32[8,64,1024]{2,1,0:T(8,128)} custom-call(bf16[4,8,2,64,128]{4,3,2,1,0:T(8,128)(2,1)S(1)} %bitcast.8, bf16[8,4,256,1024]{3,2,1,0:T(8,128)(2,1)} %constant.2.clone.t_ref), custom_call_target="tpu_custom_call" | custom-call | flops 8999999488 | bytes 24000000 | tf_op jit(solution)/shard_map/pallas_call | solution.py:356
  60.8 3.2 %copy.8 = f32[8,1,64,1024]{3,2,1,0:T(8,128)} copy(f32[8,1,64,1024]{3,2,1,0:T(8,128)} %bitcast.9) | data formatting | bytes 4194304

commit v3 on v2

v3 whole, which is shorter than its diff:
```python
import functools
import math

import jax
import jax.numpy as jnp
import ml_dtypes
import numpy as np
from jax import lax
from jax.experimental import pallas as pl
from jax.experimental.pallas import tpu as pltpu
from jax.sharding import PartitionSpec as P

LAGS = 1024
WIN = 8
BLK = 64
NY = 4
LANES = 128
MESH = pl.DeviceIdType.MESH
F32 = jnp.float32
BF16 = jnp.bfloat16

OWN, MATE, FAR, FARMATE = range(4)


def table_pieces(parts, steps, bins_total):
    fft_length = 2 * bins_total
    bins = np.arange(bins_total, dtype=np.int64)
    lags = np.arange(LAGS, dtype=np.int64) - LAGS // 2
    angles = ((bins[:, None] * lags[None, :]) % fft_length) * (2.0 * math.pi / fft_length)
    both = np.stack([np.cos(angles), -np.sin(angles)]).astype(np.float32)
    both = both.reshape(2, parts, steps, LANES, LAGS).transpose(1, 2, 0, 3, 4)
    return both.reshape(parts, steps, 2 * LANES, LAGS).astype(ml_dtypes.bfloat16)


def kernel(rows_z, steps, s_ref, t_ref, o_ref, r_in, y_buf, x_in, x_far, table, lhs, xf, acc, r_out,
           xz_sem, yz_sem, y_sem, x_sem, t_sem, xo_sem, yo_sem, xe_sem, ye_sem, ys_sem, xs_sem, ro_sem, ri_sem):
    sta = lax.axis_index("sta")
    me = lax.axis_index("freq")
    z = sta // NY
    yy = sta % NY
    chip = me // 2
    core = me % 2
    last = rows_z * NY - 1
    turn = 1 - 2 * (chip % 2)
    side = ((chip + turn + 4) % 4, (chip - turn + 4) % 4)
    across = (chip + 2) % 4
    mate = me + 1 - 2 * core

    def at(where, other):
        return 2 * where + (core + other) % 2

    x_low = z == 0
    y_high = z == rows_z - 1
    x_src = sta == 0
    y_src = sta == last
    x_pass = jnp.logical_and(x_low, yy % 2 == 1)
    y_pass = jnp.logical_and(y_high, yy % 2 == 0)
    x_half = jnp.where(yy == 1, 0, 4)
    y_half = jnp.where(yy == 2, 0, 4)

    barrier = pltpu.get_barrier_semaphore()

    def greet(row, col):
        pl.semaphore_signal(barrier, inc=1, device_id=(row, col), device_id_type=MESH)

    greet(sta, mate)
    for h in range(2):
        for other in range(2):
            greet(sta, at(side[h], other))

    @pl.when(z > 0)
    def _():
        greet(sta - NY, me)

    @pl.when(z < rows_z - 1)
    def _():
        greet(sta + NY, me)

    @pl.when(x_pass)
    def _():
        greet(0, me)

    @pl.when(jnp.logical_and(x_low, yy == 2))
    def _():
        greet(1, me)
        greet(3, me)

    @pl.when(y_pass)
    def _():
        greet(last, me)

    @pl.when(jnp.logical_and(y_high, yy == 1))
    def _():
        greet(last - 1, me)
        greet(last - 3, me)

    expected = 5
    for flag, count in ((z < rows_z - 1, 1), (z > 0, 1), (x_src, 2), (y_src, 2), (x_pass, 1), (y_pass, 1)):
        expected = expected + jnp.where(flag, count, 0)
    pl.semaphore_wait(barrier, expected)

    def remote(src, dst, send, recv, row, col):
        return pltpu.make_async_remote_copy(
            src_ref=src, dst_ref=dst, send_sem=send, recv_sem=recv,
            device_id=(row, col), device_id_type=MESH)

    def x_out(t):
        return remote(s_ref.at[t], x_in.at[OWN, t], xo_sem.at[t], xz_sem.at[t], sta + NY, me)

    def y_out(t):
        return remote(s_ref.at[t], y_buf.at[OWN, t], yo_sem.at[t], yz_sem.at[t], sta - NY, me)

    def x_edge(t, n):
        return remote(s_ref.at[t], x_in.at[OWN, t], xe_sem.at[t, n], xz_sem.at[t], 1 + 2 * n, me)

    def y_edge(t, n):
        return remote(s_ref.at[t], y_buf.at[OWN, t], ye_sem.at[t, n], yz_sem.at[t], last - 1 - 2 * n, me)

    def x_own(t):
        return pltpu.make_async_copy(s_ref.at[t], x_in.at[OWN, t], xz_sem.at[t])

    def y_own(t):
        return pltpu.make_async_copy(s_ref.at[t], y_buf.at[OWN, t], yz_sem.at[t])

    def x_relay(t):
        piece = x_in.at[OWN, t, pl.ds(x_half, 4)]
        return remote(piece, piece, xe_sem.at[t, 0], xz_sem.at[t], 2, me)

    def y_relay(t):
        piece = y_buf.at[OWN, t, pl.ds(y_half, 4)]
        return remote(piece, piece, ye_sem.at[t, 0], yz_sem.at[t], last - 2, me)

    def y_sides(t):
        return [remote(y_buf.at[OWN, t, pl.ds(4 * h, 4)], y_buf.at[FAR, t, pl.ds(4 * h, 4)], ys_sem.at[t, h],
                       y_sem.at[FAR, t], sta, at(side[h], 0)) for h in range(2)]

    def y_mate(t):
        return remote(y_buf.at[OWN, t], y_buf.at[MATE, t], ys_sem.at[t, 2], y_sem.at[MATE, t], sta, mate)

    def y_far(t):
        return remote(y_buf.at[FAR, t], y_buf.at[FARMATE, t], ys_sem.at[t, 3], y_sem.at[FARMATE, t], sta, mate)

    def x_sides(t):
        return [remote(x_in.at[OWN, t, pl.ds(2 * where, 2)], x_far.at[0, t, 2 * h + g], xs_sem.at[t, 2 * h + g],
                       x_sem.at[FAR, t], sta, at(side[h], 0))
                for h in range(2) for g, where in enumerate((side[h], across))]

    def x_mate(t):
        return remote(x_in.at[OWN, t], x_in.at[MATE, t], xs_sem.at[t, 4], x_sem.at[MATE, t], sta, mate)

    def x_hand(t):
        return remote(x_far.at[0, t, :, 1 - core], x_far.at[1, t, :, 1 - core], xs_sem.at[t, 5],
                      x_sem.at[FARMATE, t], sta, mate)

    def arrived(ref, sem):
        pltpu.make_async_copy(ref, ref, sem).wait()

    def table_copy(t, n):
        chunk = at((side[0], chip, side[1])[n // 2], 1 - n if n < 2 else n % 2)
        return pltpu.make_async_copy(t_ref.at[chunk, t], table.at[t, pl.ds(2 * LANES * n, 2 * LANES)], t_sem.at[t, n])

    def each_start(t, start):
        def go(copy):
            if start:
                copy.start()
            else:
                copy.wait_send()

        @pl.when(z < rows_z - 1)
        def _():
            go(x_out(t))

        @pl.when(z > 0)
        def _():
            go(y_out(t))

        @pl.when(x_src)
        def _():
            go(x_edge(t, 0))
            go(x_edge(t, 1))
            if start:
                x_own(t).start()

        @pl.when(y_src)
        def _():
            go(y_edge(t, 0))
            go(y_edge(t, 1))
            if start:
                y_own(t).start()

    def enter(t):
        arrived(y_buf.at[OWN, t], yz_sem.at[t])
        for copy in y_sides(t):
            copy.start()
        y_mate(t).start()

        @pl.when(y_pass)
        def _():
            y_relay(t).start()

        arrived(x_in.at[OWN, t], xz_sem.at[t])
        for copy in x_sides(t):
            copy.start()
        x_mate(t).start()

        @pl.when(x_pass)
        def _():
            x_relay(t).start()

    def second(t):
        arrived(y_buf.at[FAR, t], y_sem.at[FAR, t])
        y_far(t).start()
        arrived(x_far.at[0, t], x_sem.at[FAR, t])
        x_hand(t).start()

    def cross(t, src, g, out):
        for h in range(2):
            group = at(side[1 - h] if g else chip, 0)
            x = [(x_in[src, 2 * t + c, group] if src < FAR else x_far[src - FAR, 2 * t + c, 2 * h + g, core]).astype(F32)
                 for c in range(2)]
            xf[h, 0] = x[0]
            xf[h, 1] = x[1]
            xf[h, 2] = x[0] + x[1]

        for h in range(2):
            def body(j, carry, h=h):
                pair = []
                for k in range(2):
                    yr = y_buf[src, 2 * t, 4 * h + 2 * j + k].astype(F32).reshape(WIN, 8, LANES)
                    yi = y_buf[src, 2 * t + 1, 4 * h + 2 * j + k].astype(F32).reshape(WIN, 8, LANES)
                    pair.append((yr, yi, yr - yi))
                for a in range(8):
                    reals = []
                    imags = []
                    for yr, yi, yd in pair:
                        u = v = d = None
                        for w in range(WIN):
                            row = pl.ds(w * 8 + a, 1)
                            uw = xf[h, 0, row, :] * yr[w]
                            vw = xf[h, 1, row, :] * yi[w]
                            dw = xf[h, 2, row, :] * yd[w]
                            u = uw if u is None else u + uw
                            v = vw if v is None else v + vw
                            d = dw if d is None else d + dw
                        reals.append(u + v)
                        imags.append(d - (u - v))
                    rows = pl.ds(pl.multiple_of(a * 32 + 16 * j, 16), 16)
                    col = 2 * LANES * (src if h else (2, 3, 1, 0)[src])
                    out[h, rows, col:col + LANES] = jnp.concatenate(reals, 0).astype(BF16)
                    out[h, rows, col + LANES:col + 2 * LANES] = jnp.concatenate(imags, 0).astype(BF16)
                return carry

            lax.fori_loop(0, 2, body, 0)

    def product(t, h, left, first=0, count=4):
        cols = slice(2 * LANES * first, 2 * LANES * (first + count))
        bins = slice(2 * LANES * (2 * h + first), 2 * LANES * (2 * h + first + count))
        return jnp.dot(left[h, :, cols], table[t, bins, :], preferred_element_type=F32)

    def r_copy(h):
        return remote(r_out.at[h], r_in.at[:, h], ro_sem.at[h], ri_sem.at[h], sta, at(side[1 - h], 0))

    def all_out(u, carry):
        each_start(u, True)
        return carry

    def all_tables(t, carry):
        for n in range(6):
            table_copy(t, n).start()
        return carry

    lax.fori_loop(0, 2 * steps, all_out, 0)
    lax.fori_loop(0, steps, all_tables, 0)
    acc[...] = jnp.zeros_like(acc)
    o_ref[...] = jnp.zeros_like(o_ref)

    def near(t):
        cross(t, OWN, 1, lhs)
        for u in (2 * t, 2 * t + 1):
            arrived(y_buf.at[MATE, u], y_sem.at[MATE, u])
            arrived(x_in.at[MATE, u], x_sem.at[MATE, u])
        cross(t, MATE, 1, lhs)

    def far_mate(t):
        for u in (2 * t, 2 * t + 1):
            arrived(y_buf.at[FARMATE, u], y_sem.at[FARMATE, u])
            arrived(x_far.at[1, u, :, core], x_sem.at[FARMATE, u])
        cross(t, FARMATE, 1, lhs)

    def tables_here(t):
        for n in range(6):
            table_copy(t, n).wait()

    enter(0)
    enter(1)
    second(0)
    near(0)

    def step(t, carry):
        enter(2 * t)
        second(2 * t - 1)
        cross(t - 1, FAR, 1, lhs)
        enter(2 * t + 1)
        far_mate(t - 1)
        tables_here(t - 1)
        for h in range(2):
            acc[h] += product(t - 1, h, lhs)
        second(2 * t)
        near(t)
        return carry

    lax.fori_loop(1, steps, step, 0)

    end = steps - 1
    tables_here(end)
    second(2 * steps - 1)
    cross(end, FAR, 1, lhs)
    for h in range(2):
        acc[h] += product(end, h, lhs, 1 - h, 3)
    far_mate(end)
    for h in range(2):
        r_out[h] = (acc[h] + product(end, h, lhs, 3 * h, 1)).astype(BF16).reshape(8, 32, LAGS)
        r_copy(h).start()

    def mine(t, carry):
        for src in range(4):
            cross(t, src, 0, lhs)
        for h in range(2):
            o_ref[:, h] += product(t, h, lhs).reshape(8, 32, LAGS)
        return carry

    lax.fori_loop(0, steps, mine, 0)

    def drain(u, carry):
        each_start(u, False)

        @pl.when(x_pass)
        def _():
            x_relay(u).wait_send()

        @pl.when(y_pass)
        def _():
            y_relay(u).wait_send()

        for copy in y_sides(u) + [y_mate(u), y_far(u)] + x_sides(u) + [x_mate(u), x_hand(u)]:
            copy.wait_send()
        return carry

    lax.fori_loop(0, 2 * steps, drain, 0)
    for h in range(2):
        r_copy(h).wait()


def finish(norm, own_ref, others_ref, o_ref, buf, sem):
    def out(a):
        return pltpu.make_async_copy(buf.at[a], o_ref.at[a], sem.at[a])

    for a in range(8):
        buf[a] = (own_ref[a] + others_ref[a].astype(F32)) * norm
        out(a).start()
    for a in range(8):
        out(a).wait()


def on_device(rows_z, parts, spectra, pair_blocks):
    del pair_blocks
    bins_local = spectra.shape[3]
    steps = bins_local // LANES
    bins_total = bins_local * parts
    norm = 1.0 / math.sqrt(WIN * bins_total)
    table = jnp.asarray(table_pieces(parts, steps, bins_total))
    pieces = spectra.reshape(WIN, 8, 8, 2, steps, LANES).transpose(4, 3, 1, 0, 2, 5)
    pieces = pieces.reshape(2 * steps, 8, BLK, LANES)
    dma = pltpu.SemaphoreType.DMA
    own, others = pl.pallas_call(
        functools.partial(kernel, rows_z, steps),
        out_shape=(jax.ShapeDtypeStruct((8, 2, 32, LAGS), F32), jax.ShapeDtypeStruct((8, 2, 32, LAGS), BF16)),
        in_specs=[pl.BlockSpec(memory_space=pl.ANY)] * 2,
        out_specs=(pl.BlockSpec(memory_space=pltpu.VMEM),) * 2,
        scratch_shapes=[
            pltpu.VMEM((4, 2 * steps, 8, BLK, LANES), BF16),
            pltpu.VMEM((2, 2 * steps, 8, BLK, LANES), BF16),
            pltpu.VMEM((2, 2 * steps, 4, 2, BLK, LANES), BF16),
            pltpu.VMEM((steps, 12 * LANES, LAGS), BF16),
            pltpu.VMEM((2, 256, 8 * LANES), BF16),
            pltpu.VMEM((2, 3, BLK, LANES), F32),
            pltpu.VMEM((2, 256, LAGS), F32),
            pltpu.VMEM((2, 8, 32, LAGS), BF16),
            dma((2 * steps,)), dma((2 * steps,)), dma((4, 2 * steps)), dma((4, 2 * steps)), dma((steps, 6)),
            dma((2 * steps,)), dma((2 * steps,)), dma((2 * steps, 2)), dma((2 * steps, 2)),
            dma((2 * steps, 4)), dma((2 * steps, 6)), dma((2,)), dma((2,)),
        ],
        compiler_params=pltpu.CompilerParams(
            collective_id=0, has_side_effects=True, vmem_limit_bytes=44 * 1024 * 1024),
        cost_estimate=pl.CostEstimate(flops=9_000_000_000, bytes_accessed=24_000_000, transcendentals=0),
    )(pieces, table)
    out = pl.pallas_call(
        functools.partial(finish, norm),
        out_shape=jax.ShapeDtypeStruct((8, 2, 32, LAGS), F32),
        in_specs=[pl.BlockSpec(memory_space=pltpu.VMEM)] * 2,
        out_specs=pl.BlockSpec(memory_space=pl.ANY),
        scratch_shapes=[pltpu.VMEM((8, 2, 32, LAGS), F32), dma((8,))],
        compiler_params=pltpu.CompilerParams(vmem_limit_bytes=8 * 1024 * 1024),
    )(own, others)
    return out.reshape(8, 1, BLK, LAGS)


def solution(mesh):
    rows_z = mesh.shape["sta"] // NY
    return jax.shard_map(
        functools.partial(on_device, rows_z, mesh.shape["freq"]),
        mesh=mesh,
        in_specs=(P(None, "sta", None, "freq"), P("sta", None)),
        out_specs=P("freq", "sta", None, None),
        check_vma=False,
    )
```

time: 64.1 us -> 60.4 us (0.942)
  local copies, waits for them, and re-layouts: 5.14 us -> 2 us
  Pallas kernels: 58.8 us -> 57.9 us
    unnamed x1 -> x0, local copies, waits for them, and re-layouts: 3.16 us -> none
    pallas_call x1 -> x2, Pallas kernels: 58.8 us -> 57.9 us  [the longest x1 56.5 us: on_device(): pl.pallas_call(functools.partial(kernel, rows_z, steps), out_shape=(jax.S...]
where the time goes in v3:
time: 60.4 us; the launch traced here: 59.9 us
  Pallas kernels  57.9 us (96%)
  local copies, waits for them, and re-layouts  2 us (3%)
    pallas_call x1, Pallas kernels, on_device(): pl.pallas_call(functools.partial(kernel, rows_z, steps), out_shape=(jax.S...  56.5 us
    reshape x2, local copies, waits for them, and re-layouts, on_device(): spectra.reshape(WIN, 8, 8, 2, steps, LANES).transpose(4, 3, 1, 0, 2, 5)  2 us
    pallas_call x1, Pallas kernels, on_device(): pl.pallas_call(functools.partial(finish, norm), out_shape=jax.ShapeDtypeS...  1.41 us

profile of v3, /device:TPU:232, one launch (start us, length us, event | category | flops | bytes accessed | tf_op | source)
XLA Modules:
  0.0 59.9 jit_solution(7540067142529666048)
XLA Ops:
  0.0 1.7 %reshape.9 = bf16[8,8,8,2,4,128]{5,4,3,2,1,0:T(4,128)(2,1)S(1)} reshape(bf16[8,64,2,512]{3,2,1,0:T(2,128)(2,1)} %param.3) | data formatting | bytes 2097152 | tf_op jit(solution)/shard_map/reshape | solution.py:372
  1.7 0.3 copy.3
  2.0 56.5 %shard_map.28 = (f32[8,2,32,1024]{3,2,1,0:T(8,128)S(1)}, bf16[8,2,32,1024]{3,2,1,0:T(8,128)(2,1)S(1)}) custom-call(bf16[8,8,64,128]{3,2,1,0:T(8,128)(2,1)S(1)} %bitcast.6, bf16[8,4,256,1024]{3,2,1,0:T(8,128)(2,1)} %constant.2.clone.t_ref), custom_call_target="tpu_custom_call" | custom-call | flops 8999999488 | bytes 24000000 | tf_op jit(solution)/shard_map/pallas_call | solution.py:375
  58.5 1.4 %shard_map.29 = f32[8,2,32,1024]{3,2,1,0:T(8,128)} custom-call(f32[8,2,32,1024]{3,2,1,0:T(8,128)S(1)} %get-tuple-element.7.own_ref, bf16[8,2,32,1024]{3,2,1,0:T(8,128)(2,1)S(1)} %get-tuple-element.8.others_ref), custom_call_target="tpu_custom_call" | custom-call | tf_op jit(solution)/shard_map/pallas_call | solution.py:397

commit v4 on v3

--- a/solution.py
+++ b/solution.py
@@ -33,7 +33,7 @@
 
 
 def kernel(rows_z, steps, s_ref, t_ref, o_ref, r_in, y_buf, x_in, x_far, table, lhs, xf, acc, r_out,
-           xz_sem, yz_sem, y_sem, x_sem, t_sem, xo_sem, yo_sem, xe_sem, ye_sem, ys_sem, xs_sem, ro_sem, ri_sem):
+           xz_sem, yz_sem, xr_sem, yr_sem, y_sem, x_sem, t_sem, xo_sem, yo_sem, xe_sem, ye_sem, ys_sem, xs_sem, ro_sem, ri_sem):
     sta = lax.axis_index("sta")
     me = lax.axis_index("freq")
     z = sta // NY
@@ -111,10 +111,12 @@
         return remote(s_ref.at[t], y_buf.at[OWN, t], yo_sem.at[t], yz_sem.at[t], sta - NY, me)
 
     def x_edge(t, n):
-        return remote(s_ref.at[t], x_in.at[OWN, t], xe_sem.at[t, n], xz_sem.at[t], 1 + 2 * n, me)
+        return [remote(s_ref.at[t, pl.ds(lo, 4)], x_in.at[OWN, t, pl.ds(lo, 4)], xe_sem.at[t, 2 * n + i],
+                       (xr_sem, xz_sem)[i].at[t], 1 + 2 * n, me) for i, lo in enumerate((4 * n, 4 - 4 * n))]
 
     def y_edge(t, n):
-        return remote(s_ref.at[t], y_buf.at[OWN, t], ye_sem.at[t, n], yz_sem.at[t], last - 1 - 2 * n, me)
+        return [remote(s_ref.at[t, pl.ds(lo, 4)], y_buf.at[OWN, t, pl.ds(lo, 4)], ye_sem.at[t, 2 * n + i],
+                       (yr_sem, yz_sem)[i].at[t], last - 1 - 2 * n, me) for i, lo in enumerate((4 * n, 4 - 4 * n))]
 
     def x_own(t):
         return pltpu.make_async_copy(s_ref.at[t], x_in.at[OWN, t], xz_sem.at[t])
@@ -176,36 +178,53 @@
 
         @pl.when(x_src)
         def _():
-            go(x_edge(t, 0))
-            go(x_edge(t, 1))
+            for copy in x_edge(t, 0) + x_edge(t, 1):
+                go(copy)
             if start:
                 x_own(t).start()
 
         @pl.when(y_src)
         def _():
-            go(y_edge(t, 0))
-            go(y_edge(t, 1))
+            for copy in y_edge(t, 0) + y_edge(t, 1):
+                go(copy)
             if start:
                 y_own(t).start()
 
+    def early(t):
+        @pl.when(y_pass)
+        def _():
+            arrived(y_buf.at[OWN, t, pl.ds(0, 4)], yr_sem.at[t])
+            y_relay(t).start()
+
+        @pl.when(x_pass)
+        def _():
+            arrived(x_in.at[OWN, t, pl.ds(0, 4)], xr_sem.at[t])
+            x_relay(t).start()
+
     def enter(t):
-        arrived(y_buf.at[OWN, t], yz_sem.at[t])
+        @pl.when(y_pass)
+        def _():
+            arrived(y_buf.at[OWN, t, pl.ds(0, 4)], yz_sem.at[t])
+
+        @pl.when(jnp.logical_not(y_pass))
+        def _():
+            arrived(y_buf.at[OWN, t], yz_sem.at[t])
+
         for copy in y_sides(t):
             copy.start()
         y_mate(t).start()
 
-        @pl.when(y_pass)
-        def _():
-            y_relay(t).start()
-
-        arrived(x_in.at[OWN, t], xz_sem.at[t])
+        @pl.when(x_pass)
+        def _():
+            arrived(x_in.at[OWN, t, pl.ds(0, 4)], xz_sem.at[t])
+
+        @pl.when(jnp.logical_not(x_pass))
+        def _():
+            arrived(x_in.at[OWN, t], xz_sem.at[t])
+
         for copy in x_sides(t):
             copy.start()
         x_mate(t).start()
-
-        @pl.when(x_pass)
-        def _():
-            x_relay(t).start()
 
     def second(t):
         arrived(y_buf.at[FAR, t], y_sem.at[FAR, t])
@@ -291,14 +310,18 @@
         for n in range(6):
             table_copy(t, n).wait()
 
+    early(0)
     enter(0)
+    early(1)
     enter(1)
     second(0)
+    early(2)
     near(0)
 
     def step(t, carry):
         enter(2 * t)
         second(2 * t - 1)
+        early(2 * t + 1)
         cross(t - 1, FAR, 1, lhs)
         enter(2 * t + 1)
         far_mate(t - 1)
@@ -306,6 +329,11 @@
         for h in range(2):
             acc[h] += product(t - 1, h, lhs)
         second(2 * t)
+
+        @pl.when(t < steps - 1)
+        def _():
+            early(2 * t + 2)
+
         near(t)
         return carry
 
@@ -386,8 +414,9 @@
             pltpu.VMEM((2, 3, BLK, LANES), F32),
             pltpu.VMEM((2, 256, LAGS), F32),
             pltpu.VMEM((2, 8, 32, LAGS), BF16),
-            dma((2 * steps,)), dma((2 * steps,)), dma((4, 2 * steps)), dma((4, 2 * steps)), dma((steps, 6)),
-            dma((2 * steps,)), dma((2 * steps,)), dma((2 * steps, 2)), dma((2 * steps, 2)),
+            dma((2 * steps,)), dma((2 * steps,)), dma((2 * steps,)), dma((2 * steps,)),
+            dma((4, 2 * steps)), dma((4, 2 * steps)), dma((steps, 6)),
+            dma((2 * steps,)), dma((2 * steps,)), dma((2 * steps, 4)), dma((2 * steps, 4)),
             dma((2 * steps, 4)), dma((2 * steps, 6)), dma((2,)), dma((2,)),
         ],
         compiler_params=pltpu.CompilerParams(

time: 60.4 us -> 59.8 us (0.990)
  no operation moved by 1% of the time
where the time goes in v4:
time: 59.8 us; the launch traced here: 59.7 us
  Pallas kernels  57.7 us (96%)
  local copies, waits for them, and re-layouts  2 us (3%)
    pallas_call x1, Pallas kernels, on_device(): pl.pallas_call(functools.partial(kernel, rows_z, steps), out_shape=(jax.S...  56.3 us
    reshape x2, local copies, waits for them, and re-layouts, on_device(): spectra.reshape(WIN, 8, 8, 2, steps, LANES).transpose(4, 3, 1, 0, 2, 5)  2 us
    pallas_call x1, Pallas kernels, on_device(): pl.pallas_call(functools.partial(finish, norm), out_shape=jax.ShapeDtypeS...  1.41 us

profile of v4, /device:TPU:232, one launch (start us, length us, event | category | flops | bytes accessed | tf_op | source)
XLA Modules:
  0.0 59.7 jit_solution(11250912736335194522)
XLA Ops:
  0.0 1.7 %reshape.9 = bf16[8,8,8,2,4,128]{5,4,3,2,1,0:T(4,128)(2,1)S(1)} reshape(bf16[8,64,2,512]{3,2,1,0:T(2,128)(2,1)} %param.3) | data formatting | bytes 2097152 | tf_op jit(solution)/shard_map/reshape | solution.py:400
  1.7 0.3 copy.3
  2.0 56.3 %shard_map.28 = (f32[8,2,32,1024]{3,2,1,0:T(8,128)S(1)}, bf16[8,2,32,1024]{3,2,1,0:T(8,128)(2,1)S(1)}) custom-call(bf16[8,8,64,128]{3,2,1,0:T(8,128)(2,1)S(1)} %bitcast.6, bf16[8,4,256,1024]{3,2,1,0:T(8,128)(2,1)} %constant.2.clone.t_ref), custom_call_target="tpu_custom_call" | custom-call | flops 8999999488 | bytes 24000000 | tf_op jit(solution)/shard_map/pallas_call | solution.py:403
  58.3 1.4 %shard_map.29 = f32[8,2,32,1024]{3,2,1,0:T(8,128)} custom-call(f32[8,2,32,1024]{3,2,1,0:T(8,128)S(1)} %get-tuple-element.7.own_ref, bf16[8,2,32,1024]{3,2,1,0:T(8,128)(2,1)S(1)} %get-tuple-element.8.others_ref), custom_call_target="tpu_custom_call" | custom-call | tf_op jit(solution)/shard_map/pallas_call | solution.py:426

commit v5 on v4

--- a/solution.py
+++ b/solution.py
@@ -49,6 +49,7 @@
     def at(where, other):
         return 2 * where + (core + other) % 2
 
+    beside = [at(side[h], 0) for h in range(2)]
     x_low = z == 0
     y_high = z == rows_z - 1
     x_src = sta == 0
@@ -134,7 +135,7 @@
 
     def y_sides(t):
         return [remote(y_buf.at[OWN, t, pl.ds(4 * h, 4)], y_buf.at[FAR, t, pl.ds(4 * h, 4)], ys_sem.at[t, h],
-                       y_sem.at[FAR, t], sta, at(side[h], 0)) for h in range(2)]
+                       y_sem.at[FAR, t], sta, beside[h]) for h in range(2)]
 
     def y_mate(t):
         return remote(y_buf.at[OWN, t], y_buf.at[MATE, t], ys_sem.at[t, 2], y_sem.at[MATE, t], sta, mate)
@@ -144,7 +145,7 @@
 
     def x_sides(t):
         return [remote(x_in.at[OWN, t, pl.ds(2 * where, 2)], x_far.at[0, t, 2 * h + g], xs_sem.at[t, 2 * h + g],
-                       x_sem.at[FAR, t], sta, at(side[h], 0))
+                       x_sem.at[FAR, t], sta, beside[h])
                 for h in range(2) for g, where in enumerate((side[h], across))]
 
     def x_mate(t):
@@ -212,7 +213,6 @@
 
         for copy in y_sides(t):
             copy.start()
-        y_mate(t).start()
 
         @pl.when(x_pass)
         def _():
@@ -224,6 +224,7 @@
 
         for copy in x_sides(t):
             copy.start()
+        y_mate(t).start()
         x_mate(t).start()
 
     def second(t):
@@ -277,7 +278,7 @@
         return jnp.dot(left[h, :, cols], table[t, bins, :], preferred_element_type=F32)
 
     def r_copy(h):
-        return remote(r_out.at[h], r_in.at[:, h], ro_sem.at[h], ri_sem.at[h], sta, at(side[1 - h], 0))
+        return remote(r_out.at[h], r_in.at[:, h], ro_sem.at[h], ri_sem.at[h], sta, beside[1 - h])
 
     def all_out(u, carry):
         each_start(u, True)
@@ -397,7 +398,8 @@
     bins_total = bins_local * parts
     norm = 1.0 / math.sqrt(WIN * bins_total)
     table = jnp.asarray(table_pieces(parts, steps, bins_total))
-    pieces = spectra.reshape(WIN, 8, 8, 2, steps, LANES).transpose(4, 3, 1, 0, 2, 5)
+    rows = lax.optimization_barrier(spectra.reshape(WIN * BLK, 2 * bins_local))
+    pieces = rows.reshape(WIN, 8, 8, 2, steps, LANES).transpose(4, 3, 1, 0, 2, 5)
     pieces = pieces.reshape(2 * steps, 8, BLK, LANES)
     dma = pltpu.SemaphoreType.DMA
     own, others = pl.pallas_call(

time: 59.8 us -> 59.7 us (level)
    reshape x2 -> x0, local copies, waits for them, and re-layouts: 2 us -> none  [on_device(): spectra.reshape(WIN, 8, 8, 2, steps, LANES).transpose(4, 3, 1, 0, 2, 5)]
    unnamed x0 -> x1, local copies, waits for them, and re-layouts: none -> 1.46 us
where the time goes in v5:
time: 59.7 us; the launch traced here: 59.5 us
  Pallas kernels  57.7 us (97%)
  local copies, waits for them, and re-layouts  1.76 us (3%)
    pallas_call x1, Pallas kernels, on_device(): pl.pallas_call(functools.partial(kernel, rows_z, steps), out_shape=(jax.S...  56.3 us
    unnamed x1, local copies, waits for them, and re-layouts  1.46 us
    pallas_call x1, Pallas kernels, on_device(): pl.pallas_call(functools.partial(finish, norm), out_shape=jax.ShapeDtypeS...  1.41 us

profile of v5, /device:TPU:232, one launch (start us, length us, event | category | flops | bytes accessed | tf_op | source)
XLA Modules:
  0.0 59.5 jit_solution(11367528009581352801)
XLA Ops:
  0.0 1.5 %copy.6 = bf16[64,8,2,512]{3,1,2,0:T(8,128)(2,1)S(1)} copy(bf16[64,8,2,512]{3,2,1,0:T(2,128)(2,1)} %bitcast.12) | data formatting | bytes 2097152
  1.5 0.3 copy.4
  1.8 56.3 %shard_map.28 = (f32[8,2,32,1024]{3,2,1,0:T(8,128)S(1)}, bf16[8,2,32,1024]{3,2,1,0:T(8,128)(2,1)S(1)}) custom-call(bf16[8,8,64,128]{3,2,1,0:T(8,128)(2,1)S(1)} %bitcast.10, bf16[8,4,256,1024]{3,2,1,0:T(8,128)(2,1)} %constant.2.clone.t_ref), custom_call_target="tpu_custom_call" | custom-call | flops 8999999488 | bytes 24000000 | tf_op jit(solution)/shard_map/pallas_call | solution.py:405
  58.1 1.4 %shard_map.29 = f32[8,2,32,1024]{3,2,1,0:T(8,128)} custom-call(f32[8,2,32,1024]{3,2,1,0:T(8,128)S(1)} %get-tuple-element.7.own_ref, bf16[8,2,32,1024]{3,2,1,0:T(8,128)(2,1)S(1)} %get-tuple-element.8.others_ref), custom_call_target="tpu_custom_call" | custom-call | tf_op jit(solution)/shard_map/pallas_call | solution.py:428
